TPU v7x, 32 devices: a whole 2x2x4 slice. The times are simulated.
32 devices in a mesh: oi: 4 (over z), oj: 8 (over y, x, core).
Axes of the slice: x: 2, y: 2, z: 4, core: 2. Of those that a mesh axis runs over, the one named last changes fastest.
Arguments:
- amplitudes: bfloat16 [768, 128, 128], P(('oi', 'oj')), may hold values from -6 to 6
- exchange_ints: bfloat16 [768, 128, 128], P(('oi', 'oj')), may hold values from -6 to 6
- row_intersection: bfloat16 [768, 128, 128], P(('oi', 'oj')), may hold values from -0.5 to 0.5
- col_intersection: bfloat16 [768, 128, 128], P(('oi', 'oj')), may hold values from -0.5 to 0.5
- pno_energy: float32 [768, 128], P(('oi', 'oj')), may hold values from 0.2 to 1
- row_fock: float32 [768], P(('oi', 'oj')), may hold values from -1 to 1
- col_fock: float32 [768], P(('oi', 'oj')), may hold values from -1 to 1
- pair_occ: int32 [768, 2], P(('oi', 'oj')), may hold values from 0 to 19999
- fock_occ: float32 [20000], replicated, may hold values from -0.6 to -0.2
- row_peer: int32 [768, 1], P(('oi', 'oj')), may hold values from 0 to 7; in each aligned block of 24 rows (0 to 23, 24 to 47, ...) at most 4 rows name the same one
- row_slot: int32 [768], P(('oi', 'oj')), may hold values from 0 to 23
- col_peer: int32 [768, 1], P(('oi', 'oj')), may hold values from 0 to 3; in each aligned block of 24 rows (0 to 23, 24 to 47, ...) at most 7 rows name the same one
- col_slot: int32 [768], P(('oi', 'oj')), may hold values from 0 to 23
Outputs:
- new_amplitudes: bfloat16 [768, 128, 128], P(('oi', 'oj'))
- residual: bfloat16 [768, 128, 128], P(('oi', 'oj'))
Inputs may be any that keep to these rules, and one draw needn't show every extreme that they name: `row_peer`: among the pairs of one device no index is named by more than 4 pairs, a bound that some block reaches. `col_peer`: among the pairs of one device no index is named by more than 7 pairs, a bound that some block reaches.
All inputs are finite; a program needn't handle non-finite values.
Results may differ from a plain program's by a relative error of at most 0.012.
The roundings to bfloat16 on the way count: a program that leaves them out, or rounds other values in their place, can miss the bound.
Values may be sent and summed in bfloat16 or wider, within the bound.
A program may use at most 64 MiB of HBM per device.

v0:
```python
import jax
import jax.numpy as jnp
from jax import lax
from jax.sharding import PartitionSpec as P

ITERS = 3


def couple(blocks, intersection):
    first = jnp.einsum(
        "pab,pbc->pac", intersection, blocks, preferred_element_type=jnp.float32
    ).astype(jnp.bfloat16)
    return jnp.einsum("pac,pdc->pad", first, intersection, preferred_element_type=jnp.float32)


def layout(peer, slot, peer_count, capacity):
    marker = (peer[:, None] == jnp.arange(peer_count, dtype=jnp.int32)[None, :]).astype(jnp.int32)
    before = jnp.sum((jnp.cumsum(marker, axis=0) - marker) * marker, axis=1)
    target = peer * capacity + before
    slot_table = jnp.zeros((peer_count * capacity,), jnp.int32).at[target].set(slot)
    return (target, slot_table.reshape(peer_count, capacity))


def body(
    amplitudes,
    exchange_ints,
    row_intersection,
    col_intersection,
    pno_energy,
    row_fock,
    col_fock,
    pair_occ,
    fock_occ,
    row_peer,
    row_slot,
    col_peer,
    col_slot,
):
    pairs_here = amplitudes.shape[0]
    width = amplitudes.shape[1]
    row_count = lax.axis_size("oj")
    col_count = lax.axis_size("oi")
    row_capacity = max(2, (pairs_here + row_count - 1) // row_count + 1)
    col_capacity = max(2, (pairs_here + col_count - 1) // col_count + 1)
    row_target, row_table = layout(row_peer[:, 0], row_slot, row_count, row_capacity)
    col_target, col_table = layout(col_peer[:, 0], col_slot, col_count, col_capacity)
    matches = (
        pair_occ.reshape(-1)[:, None] == jnp.arange(fock_occ.shape[0], dtype=jnp.int32)[None, :]
    )
    picked = jnp.sum(jnp.where(matches, fock_occ[None, :], 0.0), axis=1).reshape(-1, 2)
    occupied = picked[:, 0] + picked[:, 1]
    denominator = pno_energy[:, :, None] + pno_energy[:, None, :] - occupied[:, None, None]
    ints_wide = exchange_ints.astype(jnp.float32)
    row_wanted = lax.all_to_all(row_table, "oj", split_axis=0, concat_axis=0, tiled=True)
    col_wanted = lax.all_to_all(col_table, "oi", split_axis=0, concat_axis=0, tiled=True)
    current = amplitudes
    residual = jnp.zeros(amplitudes.shape, jnp.float32)
    for sweep in range(ITERS):
        row_fetched = lax.all_to_all(
            current[row_wanted], "oj", split_axis=0, concat_axis=0, tiled=True
        )
        col_fetched = lax.all_to_all(
            current[col_wanted], "oi", split_axis=0, concat_axis=0, tiled=True
        )
        row_term = couple(row_fetched.reshape(-1, width, width)[row_target], row_intersection)
        col_term = couple(col_fetched.reshape(-1, width, width)[col_target], col_intersection)
        own_wide = current.astype(jnp.float32)
        residual = (
            ints_wide
            + denominator * own_wide
            - row_fock[:, None, None] * row_term
            - col_fock[:, None, None] * col_term
        )
        current = (own_wide - residual / denominator).astype(jnp.bfloat16)
    return (current, residual.astype(jnp.bfloat16))


def solution(mesh):
    return jax.shard_map(
        body,
        mesh=mesh,
        in_specs=(
            P(("oi", "oj"), None, None),
            P(("oi", "oj"), None, None),
            P(("oi", "oj"), None, None),
            P(("oi", "oj"), None, None),
            P(("oi", "oj"), None),
            P(("oi", "oj")),
            P(("oi", "oj")),
            P(("oi", "oj"), None),
            P(),
            P(("oi", "oj"), None),
            P(("oi", "oj")),
            P(("oi", "oj"), None),
            P(("oi", "oj")),
        ),
        out_specs=(P(("oi", "oj"), None, None), P(("oi", "oj"), None, None)),
        check_vma=False,
    )
```

profile of v0, /device:TPU:0, one launch (start us, length us, event | category | flops | bytes accessed | tf_op | source)
XLA Modules:
  0.0 180.1 jit_solution(513200580543514590)
XLA Ops:
  4.5 5.2 %all-to-all-start = ((s32[8,1,4]{2,1,0:T(1,128)}), s32[8,1,4]{2,1,0:T(1,128)S(1)}, u32[]{:S(2)}, u32[]{:S(2)}) async-start(s32[8,1,4]{2,1,0:T(1,128)} %bitcast.3), calls=%async_computation | async-start | bytes 8192 | tf_op jit(solution)/shard_map/all_to_all | solution.py:54
  14.2 4.9 %all-to-all-start.2 = ((s32[4,1,7]{2,1,0:T(1,128)}), s32[4,1,7]{2,1,0:T(1,128)S(1)}, u32[]{:S(2)}, u32[]{:S(2)}) async-start(s32[4,1,7]{2,1,0:T(1,128)} %bitcast.10), calls=%async_computation.2 | async-start | bytes 4096 | tf_op jit(solution)/shard_map/all_to_all | solution.py:55
  19.3 2.8 %gather_fusion = bf16[32,128,128]{2,1,0:T(8,128)(2,1)} fusion(bf16[24,128,128]{2,1,0:T(8,128)(2,1)} %param.13, s32[1024]{0:T(1024)S(1)} %pad_clamp_fusion.3), kind=kCustom, calls=%fused_computation | custom fusion | bytes 2097280 | tf_op jit(solution)/shard_map/gather | solution.py:60
  22.1 2.4 %all-to-all-done.2 = s32[4,1,7]{2,1,0:T(1,128)S(1)} async-done(((s32[4,1,7]{2,1,0:T(1,128)}), s32[4,1,7]{2,1,0:T(1,128)S(1)}, u32[]{:S(2)}, u32[]{:S(2)}) %all-to-all-start.2) | async-done | bytes 144 | tf_op jit(solution)/shard_map/all_to_all | solution.py:55
  24.5 3.6 %all-to-all-start.1 = ((bf16[8,4,128,128]{3,2,1,0:T(8,128)(2,1)}), bf16[8,4,128,128]{3,2,1,0:T(8,128)(2,1)S(1)}, u32[]{:S(2)}, u32[]{:S(2)}) async-start(bf16[8,4,128,128]{3,2,1,0:T(8,128)(2,1)} %bitcast.5), calls=%async_computation.1 | async-start | bytes 2097152 | tf_op jit(solution)/shard_map/all_to_all | solution.py:59
  28.2 1.6 gather_fusion.2
  29.8 13.6 %all-to-all-done.1 = bf16[8,4,128,128]{3,2,1,0:T(8,128)(2,1)S(1)} async-done(((bf16[8,4,128,128]{3,2,1,0:T(8,128)(2,1)}), bf16[8,4,128,128]{3,2,1,0:T(8,128)(2,1)S(1)}, u32[]{:S(2)}, u32[]{:S(2)}) %all-to-all-start.1) | async-done | bytes 1048608 | tf_op jit(solution)/shard_map/all_to_all | solution.py:59
  43.5 4.3 %all-to-all-start.3 = ((bf16[4,7,128,128]{3,2,1,0:T(8,128)(2,1)}), bf16[4,7,128,128]{3,2,1,0:T(8,128)(2,1)}, u32[]{:S(2)}, u32[]{:S(2)}) async-start(bf16[4,7,128,128]{3,2,1,0:T(8,128)(2,1)} %bitcast.12), calls=%async_computation.3 | async-start | bytes 1835008 | tf_op jit(solution)/shard_map/all_to_all | solution.py:62
  49.1 1.6 gather_fusion.1
  50.7 3.5 %fusion.11 = f32[24,128,128]{2,1,0:T(8,128)} fusion(bf16[24,128,128]{2,1,0:T(8,128)(2,1)S(1)} %copy-done.1, bf16[24,128,128]{2,1,0:T(8,128)(2,1)} %gather_fusion.1), kind=kOutput, calls=%fused_computation.43 | convolution fusion | flops 201719808 | bytes 3145728 | tf_op jit(solution)/shard_map/pac,pdc->pad/dot_general | solution.py:13
  54.2 14.0 %all-to-all-done.3 = bf16[4,7,128,128]{3,2,1,0:T(8,128)(2,1)} async-done(((bf16[4,7,128,128]{3,2,1,0:T(8,128)(2,1)}), bf16[4,7,128,128]{3,2,1,0:T(8,128)(2,1)}, u32[]{:S(2)}, u32[]{:S(2)}) %all-to-all-start.3) | async-done | bytes 917536 | tf_op jit(solution)/shard_map/all_to_all | solution.py:62
  68.2 2.7 %gather_fusion.3 = bf16[24,128,128]{2,1,0:T(8,128)(2,1)} fusion(bf16[28,128,128]{2,1,0:T(8,128)(2,1)} %bitcast.13, s32[1024]{0:T(1024)S(1)} %pad_clamp_fusion), kind=kCustom, calls=%fused_computation.3 | custom fusion | bytes 1572960 | tf_op jit(solution)/shard_map/gather | solution.py:66
  71.0 3.5 %fusion = bf16[24,128,128]{2,1,0:T(8,128)(2,1)S(1)} fusion(bf16[24,128,128]{2,1,0:T(8,128)(2,1)S(1)} %copy-done.2, bf16[24,128,128]{2,1,0:T(8,128)(2,1)} %param.14, f32[24,128,128]{2,1,0:T(8,128)} %fusion.11, bf16[24,128,128]{2,1,0:T(8,128)(2,1)S(1)} %copy-done, bf16[24,128,128]{2,1,0:T(8,128)(2,1)} %gather_fusion.3, f32[24]{0:T(128)S(1)} %copy-done.7, ...), kind=kOutput, calls=%fused_computation.25 | convolution fusion | flops 206831616 | bytes 5517600 | tf_op jit(solution)/shard_map/pac,pdc->pad/dot_general | solution.py:13
  74.5 1.7 gather_fusion.4
  76.1 4.9 %all-to-all-start.4 = ((bf16[8,4,128,128]{3,2,1,0:T(8,128)(2,1)}), bf16[8,4,128,128]{3,2,1,0:T(8,128)(2,1)}, u32[]{:S(2)}, u32[]{:S(2)}) async-start(bf16[8,4,128,128]{3,2,1,0:T(8,128)(2,1)} %bitcast.55), calls=%async_computation.4 | async-start | bytes 2097152 | tf_op jit(solution)/shard_map/all_to_all | solution.py:59
  81.0 1.6 gather_fusion.6
  82.6 13.9 %all-to-all-done.4 = bf16[8,4,128,128]{3,2,1,0:T(8,128)(2,1)} async-done(((bf16[8,4,128,128]{3,2,1,0:T(8,128)(2,1)}), bf16[8,4,128,128]{3,2,1,0:T(8,128)(2,1)}, u32[]{:S(2)}, u32[]{:S(2)}) %all-to-all-start.4) | async-done | bytes 1048608 | tf_op jit(solution)/shard_map/all_to_all | solution.py:59
  96.5 4.2 %all-to-all-start.5 = ((bf16[4,7,128,128]{3,2,1,0:T(8,128)(2,1)}), bf16[4,7,128,128]{3,2,1,0:T(8,128)(2,1)}, u32[]{:S(2)}, u32[]{:S(2)}) async-start(bf16[4,7,128,128]{3,2,1,0:T(8,128)(2,1)} %bitcast.56), calls=%async_computation.5 | async-start | bytes 1835008 | tf_op jit(solution)/shard_map/all_to_all | solution.py:62
  100.8 1.9 %gather_fusion.5 = bf16[24,128,128]{2,1,0:T(8,128)(2,1)S(1)} fusion(bf16[32,128,128]{2,1,0:T(8,128)(2,1)} %bitcast.15, s32[1024]{0:T(1024)S(1)} %pad_clamp_fusion.2), kind=kCustom, calls=%fused_computation.5 | custom fusion | bytes 1572960 | tf_op jit(solution)/shard_map/gather | solution.py:65
  102.7 2.4 %fusion.12 = f32[24,128,128]{2,1,0:T(8,128)} fusion(bf16[24,128,128]{2,1,0:T(8,128)(2,1)S(1)} %copy-done.1, bf16[24,128,128]{2,1,0:T(8,128)(2,1)S(1)} %gather_fusion.5), kind=kOutput, calls=%fused_computation.44 | convolution fusion | flops 201719808 | bytes 3145728 | tf_op jit(solution)/shard_map/pac,pdc->pad/dot_general | solution.py:13
  105.1 16.1 %all-to-all-done.5 = bf16[4,7,128,128]{3,2,1,0:T(8,128)(2,1)} async-done(((bf16[4,7,128,128]{3,2,1,0:T(8,128)(2,1)}), bf16[4,7,128,128]{3,2,1,0:T(8,128)(2,1)}, u32[]{:S(2)}, u32[]{:S(2)}) %all-to-all-start.5) | async-done | bytes 917536 | tf_op jit(solution)/shard_map/all_to_all | solution.py:62
  121.1 2.7 %gather_fusion.7 = bf16[24,128,128]{2,1,0:T(8,128)(2,1)} fusion(bf16[28,128,128]{2,1,0:T(8,128)(2,1)} %bitcast.17, s32[1024]{0:T(1024)S(1)} %pad_clamp_fusion), kind=kCustom, calls=%fused_computation.7 | custom fusion | bytes 1572960 | tf_op jit(solution)/shard_map/gather | solution.py:66
  123.9 3.5 %fusion.1 = bf16[24,128,128]{2,1,0:T(8,128)(2,1)S(1)} fusion(bf16[24,128,128]{2,1,0:T(8,128)(2,1)S(1)} %fusion, bf16[24,128,128]{2,1,0:T(8,128)(2,1)} %param.14, f32[24,128,128]{2,1,0:T(8,128)} %fusion.12, bf16[24,128,128]{2,1,0:T(8,128)(2,1)S(1)} %copy-done, bf16[24,128,128]{2,1,0:T(8,128)(2,1)} %gather_fusion.7, f32[24]{0:T(128)S(1)} %copy-done.7, ...), kind=kOutput, calls=%fused_computation.26 | convolution fusion | flops 206831616 | bytes 5517600 | tf_op jit(solution)/shard_map/pac,pdc->pad/dot_general | solution.py:13
  127.4 1.6 gather_fusion.8
  129.0 4.9 %all-to-all-start.6 = ((bf16[8,4,128,128]{3,2,1,0:T(8,128)(2,1)}), bf16[8,4,128,128]{3,2,1,0:T(8,128)(2,1)S(1)}, u32[]{:S(2)}, u32[]{:S(2)}) async-start(bf16[8,4,128,128]{3,2,1,0:T(8,128)(2,1)} %bitcast.18), calls=%async_computation.6 | async-start | bytes 2097152 | tf_op jit(solution)/shard_map/all_to_all | solution.py:59
  133.9 1.6 gather_fusion.10
  135.5 13.8 %all-to-all-done.6 = bf16[8,4,128,128]{3,2,1,0:T(8,128)(2,1)S(1)} async-done(((bf16[8,4,128,128]{3,2,1,0:T(8,128)(2,1)}), bf16[8,4,128,128]{3,2,1,0:T(8,128)(2,1)S(1)}, u32[]{:S(2)}, u32[]{:S(2)}) %all-to-all-start.6) | async-done | bytes 1048608 | tf_op jit(solution)/shard_map/all_to_all | solution.py:59
  149.3 4.2 %all-to-all-start.7 = ((bf16[4,7,128,128]{3,2,1,0:T(8,128)(2,1)}), bf16[4,7,128,128]{3,2,1,0:T(8,128)(2,1)}, u32[]{:S(2)}, u32[]{:S(2)}) async-start(bf16[4,7,128,128]{3,2,1,0:T(8,128)(2,1)} %bitcast.20), calls=%async_computation.7 | async-start | bytes 1835008 | tf_op jit(solution)/shard_map/all_to_all | solution.py:62
  155.1 3.5 %fusion.13 = f32[24,128,128]{2,1,0:T(8,128)} fusion(bf16[24,128,128]{2,1,0:T(8,128)(2,1)S(1)} %copy-done.1, bf16[24,128,128]{2,1,0:T(8,128)(2,1)} %gather_fusion.9), kind=kOutput, calls=%fused_computation.45 | convolution fusion | flops 201719808 | bytes 3145728 | tf_op jit(solution)/shard_map/pac,pdc->pad/dot_general | solution.py:13
  158.6 15.4 %all-to-all-done.7 = bf16[4,7,128,128]{3,2,1,0:T(8,128)(2,1)} async-done(((bf16[4,7,128,128]{3,2,1,0:T(8,128)(2,1)}), bf16[4,7,128,128]{3,2,1,0:T(8,128)(2,1)}, u32[]{:S(2)}, u32[]{:S(2)}) %all-to-all-start.7) | async-done | bytes 917536 | tf_op jit(solution)/shard_map/all_to_all | solution.py:62
  174.0 1.9 %gather_fusion.11 = bf16[24,128,128]{2,1,0:T(8,128)(2,1)S(1)} fusion(bf16[28,128,128]{2,1,0:T(8,128)(2,1)} %bitcast.21, s32[1024]{0:T(1024)S(1)} %pad_clamp_fusion), kind=kCustom, calls=%fused_computation.11 | custom fusion | bytes 1572960 | tf_op jit(solution)/shard_map/gather | solution.py:66
  175.9 4.2 %fusion.23 = (bf16[24,128,128]{2,1,0:T(8,128)(2,1)}, bf16[24,128,128]{2,1,0:T(8,128)(2,1)}) fusion(f32[24]{0:T(128)S(1)} %fusion.14, f32[24,128]{1,0:T(8,128)S(1)} %copy-done.6, bf16[24,128,128]{2,1,0:T(8,128)(2,1)S(1)} %fusion.1, bf16[24,128,128]{2,1,0:T(8,128)(2,1)S(1)} %copy-done, bf16[24,128,128]{2,1,0:T(8,128)(2,1)S(1)} %gather_fusion.11, ...), kind=kOutput, calls=%fused_computation.70 | convolution fusion | flops 207224832 | bytes 6304032 | tf_op jit(solution)/shard_map/pac,pdc->pad/dot_general | solution.py:13
  (47 shorter events, 11.6 us)
Async XLA Ops:
  0.6 70.3 %copy-start = (bf16[24,128,128]{2,1,0:T(8,128)(2,1)S(1)}, bf16[24,128,128]{2,1,0:T(8,128)(2,1)}, u32[]{:S(2)}) copy-start(bf16[24,128,128]{2,1,0:T(8,128)(2,1)} %param.16) | copy-start | bytes 2359300
  4.5 9.8 %all-to-all-start = ((s32[8,1,4]{2,1,0:T(1,128)}), s32[8,1,4]{2,1,0:T(1,128)S(1)}, u32[]{:S(2)}, u32[]{:S(2)}) async-start(s32[8,1,4]{2,1,0:T(1,128)} %bitcast.3), calls=%async_computation | async-start | bytes 8192 | tf_op jit(solution)/shard_map/all_to_all | solution.py:54
  14.2 10.3 %all-to-all-start.2 = ((s32[4,1,7]{2,1,0:T(1,128)}), s32[4,1,7]{2,1,0:T(1,128)S(1)}, u32[]{:S(2)}, u32[]{:S(2)}) async-start(s32[4,1,7]{2,1,0:T(1,128)} %bitcast.10), calls=%async_computation.2 | async-start | bytes 4096 | tf_op jit(solution)/shard_map/all_to_all | solution.py:55
  22.1 6.1 %copy-start.2 = (bf16[24,128,128]{2,1,0:T(8,128)(2,1)S(1)}, bf16[24,128,128]{2,1,0:T(8,128)(2,1)}, u32[]{:S(2)}) copy-start(bf16[24,128,128]{2,1,0:T(8,128)(2,1)} %param.13) | copy-start | bytes 2359300
  24.5 18.9 %all-to-all-start.1 = ((bf16[8,4,128,128]{3,2,1,0:T(8,128)(2,1)}), bf16[8,4,128,128]{3,2,1,0:T(8,128)(2,1)S(1)}, u32[]{:S(2)}, u32[]{:S(2)}) async-start(bf16[8,4,128,128]{3,2,1,0:T(8,128)(2,1)} %bitcast.5), calls=%async_computation.1 | async-start | bytes 2097152 | tf_op jit(solution)/shard_map/all_to_all | solution.py:59
  28.2 19.6 %copy-start.4 = (s32[24,2]{0,1:T(2,128)S(1)}, s32[24,2]{0,1:T(2,128)}, u32[]{:S(2)}) copy-start(s32[24,2]{0,1:T(2,128)} %param.20) | copy-start | bytes 580
  28.2 19.8 %copy-start.3 = (f32[20000]{0:T(1024)S(1)}, f32[20000]{0:T(1024)}, u32[]{:S(2)}) copy-start(f32[20000]{0:T(1024)} %param.21) | copy-start | bytes 240004
  43.5 7.2 %copy-start.1 = (bf16[24,128,128]{2,1,0:T(8,128)(2,1)S(1)}, bf16[24,128,128]{2,1,0:T(8,128)(2,1)}, u32[]{:S(2)}) copy-start(bf16[24,128,128]{2,1,0:T(8,128)(2,1)} %param.15) | copy-start | bytes 2359300
  43.5 24.7 %all-to-all-start.3 = ((bf16[4,7,128,128]{3,2,1,0:T(8,128)(2,1)}), bf16[4,7,128,128]{3,2,1,0:T(8,128)(2,1)}, u32[]{:S(2)}, u32[]{:S(2)}) async-start(bf16[4,7,128,128]{3,2,1,0:T(8,128)(2,1)} %bitcast.12), calls=%async_computation.3 | async-start | bytes 1835008 | tf_op jit(solution)/shard_map/all_to_all | solution.py:62
  54.2 16.8 %copy-start.6 = (f32[24,128]{1,0:T(8,128)S(1)}, f32[24,128]{1,0:T(8,128)}, u32[]{:S(2)}) copy-start(f32[24,128]{1,0:T(8,128)} %param.17) | copy-start | bytes 36868
  54.2 16.8 %copy-start.7 = (f32[24]{0:T(128)S(1)}, f32[24]{0:T(128)}, u32[]{:S(2)}) copy-start(f32[24]{0:T(128)} %param.19) | copy-start | bytes 292
  54.2 16.8 %copy-start.8 = (f32[24]{0:T(128)S(1)}, f32[24]{0:T(128)}, u32[]{:S(2)}) copy-start(f32[24]{0:T(128)} %param.18) | copy-start | bytes 292
  76.1 20.4 %all-to-all-start.4 = ((bf16[8,4,128,128]{3,2,1,0:T(8,128)(2,1)}), bf16[8,4,128,128]{3,2,1,0:T(8,128)(2,1)}, u32[]{:S(2)}, u32[]{:S(2)}) async-start(bf16[8,4,128,128]{3,2,1,0:T(8,128)(2,1)} %bitcast.55), calls=%async_computation.4 | async-start | bytes 2097152 | tf_op jit(solution)/shard_map/all_to_all | solution.py:59
  96.5 24.6 %all-to-all-start.5 = ((bf16[4,7,128,128]{3,2,1,0:T(8,128)(2,1)}), bf16[4,7,128,128]{3,2,1,0:T(8,128)(2,1)}, u32[]{:S(2)}, u32[]{:S(2)}) async-start(bf16[4,7,128,128]{3,2,1,0:T(8,128)(2,1)} %bitcast.56), calls=%async_computation.5 | async-start | bytes 1835008 | tf_op jit(solution)/shard_map/all_to_all | solution.py:62
  129.0 20.3 %all-to-all-start.6 = ((bf16[8,4,128,128]{3,2,1,0:T(8,128)(2,1)}), bf16[8,4,128,128]{3,2,1,0:T(8,128)(2,1)S(1)}, u32[]{:S(2)}, u32[]{:S(2)}) async-start(bf16[8,4,128,128]{3,2,1,0:T(8,128)(2,1)} %bitcast.18), calls=%async_computation.6 | async-start | bytes 2097152 | tf_op jit(solution)/shard_map/all_to_all | solution.py:59
  149.3 24.7 %all-to-all-start.7 = ((bf16[4,7,128,128]{3,2,1,0:T(8,128)(2,1)}), bf16[4,7,128,128]{3,2,1,0:T(8,128)(2,1)}, u32[]{:S(2)}, u32[]{:S(2)}) async-start(bf16[4,7,128,128]{3,2,1,0:T(8,128)(2,1)} %bitcast.20), calls=%async_computation.7 | async-start | bytes 1835008 | tf_op jit(solution)/shard_map/all_to_all | solution.py:62
  158.6 17.3 %copy-start.5 = (bf16[24,128,128]{2,1,0:T(8,128)(2,1)S(1)}, bf16[24,128,128]{2,1,0:T(8,128)(2,1)}, u32[]{:S(2)}) copy-start(bf16[24,128,128]{2,1,0:T(8,128)(2,1)} %param.14) | copy-start | bytes 2359300
where the time goes:
time: 182 us; the launch traced here: 180 us
  waiting for transfers between devices  90.1 us (50%)
  starting transfers between devices  36.2 us (20%)
  local copies, waits for them, and re-layouts  26.8 us (15%)
  matrix products  20.5 us (11%)
  other arithmetic  5.63 us (3%)
    all_to_all x3, waiting for transfers between devices, body(): lax.all_to_all(current[col_wanted], 'oi', split_axis=0, concat_axis=0, ti...  45.5 us
    all_to_all x3, waiting for transfers between devices, body(): lax.all_to_all(current[row_wanted], 'oj', split_axis=0, concat_axis=0, ti...  41.3 us
    dot_general x6, matrix products, couple(): jnp.einsum('pac,pdc->pad', first, intersection, preferred_element_type=jn...  20.5 us
    all_to_all x3, starting transfers between devices, body(): lax.all_to_all(current[row_wanted], 'oj', split_axis=0, concat_axis=0, ti...  13.3 us
    all_to_all x3, starting transfers between devices, body(): lax.all_to_all(current[col_wanted], 'oi', split_axis=0, concat_axis=0, ti...  12.8 us
    gather x3, local copies, waits for them, and re-layouts, body(): col_fetched.reshape(-1, width, width)[col_target]  7.33 us
    gather x3, local copies, waits for them, and re-layouts, body(): current[row_wanted]  6.12 us
    all_to_all x1, starting transfers between devices, body(): lax.all_to_all(row_table, 'oj', split_axis=0, concat_axis=0, tiled=True)  5.17 us
  transfers between devices with their start and end apart: 8, of which 8 were waited for; matrix products, arithmetic and copies ran while one was open for 15% of the time, Pallas kernels for 0%

commit v1 on v0

v1 whole, which is shorter than its diff:
```python
import functools
import jax
import jax.numpy as jnp
from jax import lax
from jax.experimental import pallas as pl
from jax.experimental.pallas import tpu as pltpu
from jax.sharding import PartitionSpec as P

ITERS = 3
LANES = 128
PERM, PLACE, ROW_FROM = 0, 1, 2


def flip(me, step):
    out = me
    bit = 1
    while bit <= step:
        if step & bit:
            out = out + bit * (1 - 2 * ((me // bit) % 2))
        bit *= 2
    return out


def plan_kernel(
    rows, cols, row_cap, col_cap, row_peer, row_slot, col_peer, col_slot, table, meta, count
):
    pairs = row_peer.shape[0]
    row_me, col_me = lax.axis_index("oj"), lax.axis_index("oi")
    for g in range(rows + cols):
        count[g] = 0
        for t in range(row_cap if g < rows else col_cap):
            table[g, 0, t] = 0
    for k in range(cols * col_cap):
        meta[PERM, k] = 0
        meta[ROW_FROM, k] = 0

    @pl.loop(0, pairs)
    def _(p):
        g = row_peer[p] ^ row_me
        t = count[g]
        count[g] = t + 1
        table[g, 0, t] = row_slot[p]
        h = col_peer[p] ^ col_me
        u = count[rows + h]
        count[rows + h] = u + 1
        table[rows + h, 0, u] = col_slot[p]
        place = h * col_cap + u
        meta[PERM, place] = p
        meta[PLACE, p] = place
        meta[ROW_FROM, place] = g * row_cap + t


def sweep_kernel(
    rows,
    cols,
    row_cap,
    col_cap,
    table,
    amps,
    meta,
    row_fock,
    col_fock,
    pair_occ,
    fock_hbm,
    ints_hbm,
    row_over_hbm,
    col_over_hbm,
    energy,
    new_out,
    res_out,
    fock,
    ints,
    row_over,
    col_over,
    want_in,
    want,
    denom,
    inverse,
    partial,
    current,
    res_sorted,
    row_got_0,
    row_got_1,
    row_got_2,
    col_got,
    row_send,
    col_send,
    local_sem,
    table_send_sem,
    table_recv_sem,
    send_sem,
    recv_sem,
):
    row_got = (row_got_0, row_got_1, row_got_2)
    places = cols * col_cap
    pairs = amps.shape[0]
    width = amps.shape[1]
    row_me, col_me = lax.axis_index("oj"), lax.axis_index("oi")
    groups = [g for g in range(rows + cols) if g not in (0, rows)]

    def peer(g):
        if g < rows:
            return {"oj": flip(row_me, g)}
        return {"oi": flip(col_me, g - rows)}

    loads = [
        pltpu.make_async_copy(source, target, local_sem.at[i])
        for i, (source, target) in enumerate(
            [
                (ints_hbm, ints),
                (row_over_hbm, row_over),
                (col_over_hbm, col_over),
                (fock_hbm, fock),
            ]
        )
    ]
    barrier = pltpu.get_barrier_semaphore()
    for g in groups:
        pl.semaphore_signal(
            barrier, inc=1, device_id=peer(g), device_id_type=pl.DeviceIdType.MESH
        )
    for load in loads:
        load.start()
    want_in[0] = table[0]
    want_in[rows] = table[rows]
    pl.semaphore_wait(barrier, len(groups))
    asks = []
    for g in groups:
        ask = pltpu.make_async_remote_copy(
            src_ref=table.at[g],
            dst_ref=want_in.at[g],
            send_sem=table_send_sem.at[g],
            recv_sem=table_recv_sem.at[g],
            device_id=peer(g),
            device_id_type=pl.DeviceIdType.MESH,
        )
        ask.start()
        asks.append(ask)
    for ask in asks:
        ask.wait()
    move = pltpu.make_async_copy(want_in, want, local_sem.at[4])
    move.start()
    move.wait()

    def block_copy(sweep, g):
        if g < rows:
            here = pl.ds(g * row_cap, row_cap)
            source, target = row_send.at[sweep, here], row_got[sweep].at[here]
        else:
            here = pl.ds((g - rows) * col_cap, col_cap)
            source, target = col_send.at[sweep, here], col_got.at[sweep, here]
        return pltpu.make_async_remote_copy(
            src_ref=source,
            dst_ref=target,
            send_sem=send_sem.at[sweep, g],
            recv_sem=recv_sem.at[sweep, g],
            device_id=peer(g),
            device_id_type=pl.DeviceIdType.MESH,
        )

    def dot(a, b, contract):
        return lax.dot_general(
            a, b, (((1,), (contract,)), ((), ())), preferred_element_type=jnp.float32
        )

    def couple(blocks, overs):
        firsts = [dot(o, b, 0).astype(jnp.bfloat16) for o, b in zip(overs, blocks)]
        return [dot(f, o, 1) for f, o in zip(firsts, overs)]

    order = list(range(rows + cols - 1, rows, -1)) + list(range(rows - 1, 0, -1)) + [rows, 0]
    for sweep in range(ITERS):
        held = (sweep + 1) % 2

        def taken(slot):
            if sweep == 0:
                return amps[slot]
            return current[held, meta[PLACE, slot]]

        for g in order:
            if g < rows:
                first, cap, out, got = g * row_cap, row_cap, row_send, row_got[sweep]
            else:
                first, cap, out, got = (g - rows) * col_cap, col_cap, col_send, col_got.at[sweep]
            out = got if g in (0, rows) else out.at[sweep]
            for t in range(cap):
                out[first + t] = taken(want[g, 0, t])
            if g not in (0, rows):
                block_copy(sweep, g).start()

        if sweep == 0:
            for load in loads:
                load.wait()

            @pl.loop(0, places)
            def _(k):
                p = meta[PERM, k]
                occupied = fock[pair_occ[2 * p]] + fock[pair_occ[2 * p + 1]]
                across = jnp.broadcast_to(energy[p], (width, width))
                value = across + across.T - occupied
                denom[k] = value
                inverse[k] = 1.0 / value

        for g in range(1, rows):
            block_copy(sweep, g).wait_recv()

        @pl.loop(0, cols)
        def _(h):
            at = [h * col_cap + t for t in range(col_cap)]
            who = [meta[PERM, k] for k in at]
            overs = [row_over[p] for p in who]
            blocks = [row_got[sweep][meta[ROW_FROM, k]] for k in at]
            for k, p, term in zip(at, who, couple(blocks, overs)):
                partial[k] = row_fock[p] * term - ints[p].astype(jnp.float32)

        def col_group(h):
            at = [h * col_cap + t for t in range(col_cap)]
            who = [meta[PERM, k] for k in at]
            overs = [col_over[p] for p in who]
            blocks = [col_got[sweep, k] for k in at]
            for k, p, term in zip(at, who, couple(blocks, overs)):
                total = partial[k] + col_fock[p] * term
                if sweep == ITERS - 1:
                    own = current[held, k].astype(jnp.float32)
                    res_sorted[k] = (denom[k] * own - total).astype(jnp.bfloat16)
                current[sweep % 2, k] = (total * inverse[k]).astype(jnp.bfloat16)

        col_group(0)

        @pl.loop(1, cols)
        def _(h):
            here = pl.ds(h * col_cap, col_cap)
            pltpu.make_async_remote_copy(
                src_ref=col_send.at[sweep, here],
                dst_ref=col_got.at[sweep, here],
                send_sem=send_sem.at[sweep, rows + h],
                recv_sem=recv_sem.at[sweep, rows + h],
                device_id={"oi": flip(col_me, 1)},
                device_id_type=pl.DeviceIdType.MESH,
            ).wait_recv()
            col_group(h)

    for p in range(pairs):
        place = meta[PLACE, p]
        new_out[p] = current[(ITERS - 1) % 2, place]
        res_out[p] = res_sorted[place]
    for sweep in range(ITERS):
        for g in groups:
            block_copy(sweep, g).wait_send()


def body(
    amplitudes,
    exchange_ints,
    row_intersection,
    col_intersection,
    pno_energy,
    row_fock,
    col_fock,
    pair_occ,
    fock_occ,
    row_peer,
    row_slot,
    col_peer,
    col_slot,
):
    pairs, width, _ = amplitudes.shape
    rows, cols = lax.axis_size("oj"), lax.axis_size("oi")
    row_cap = max(2, (pairs + rows - 1) // rows + 1)
    col_cap = max(2, (pairs + cols - 1) // cols + 1)
    places = cols * col_cap
    smem = pl.BlockSpec(memory_space=pltpu.SMEM)
    vmem = pl.BlockSpec(memory_space=pltpu.VMEM)
    anywhere = pl.BlockSpec(memory_space=pl.ANY)
    table, meta = pl.pallas_call(
        functools.partial(plan_kernel, rows, cols, row_cap, col_cap),
        out_shape=(
            jax.ShapeDtypeStruct((rows + cols, 1, LANES), jnp.int32),
            jax.ShapeDtypeStruct((3, LANES), jnp.int32),
        ),
        in_specs=[smem] * 4,
        out_specs=(smem, smem),
        scratch_shapes=[pltpu.SMEM((rows + cols,), jnp.int32)],
        name="plan",
    )(row_peer.reshape(-1), row_slot, col_peer.reshape(-1), col_slot)
    wide = jax.ShapeDtypeStruct(amplitudes.shape, jnp.bfloat16)
    block = (width, width)
    half, full = jnp.bfloat16, jnp.float32
    return pl.pallas_call(
        functools.partial(sweep_kernel, rows, cols, row_cap, col_cap),
        out_shape=(wide, wide),
        in_specs=[vmem, vmem, smem, smem, smem, smem, anywhere, anywhere, anywhere, anywhere, vmem],
        out_specs=(vmem, vmem),
        scratch_shapes=[
            pltpu.SMEM(fock_occ.shape, full),
            pltpu.VMEM(amplitudes.shape, half),
            pltpu.VMEM(amplitudes.shape, half),
            pltpu.VMEM(amplitudes.shape, half),
            pltpu.VMEM((rows + cols, 1, LANES), jnp.int32),
            pltpu.SMEM((rows + cols, 1, LANES), jnp.int32),
            pltpu.VMEM((places,) + block, full),
            pltpu.VMEM((places,) + block, full),
            pltpu.VMEM((places,) + block, full),
            pltpu.VMEM((2, places) + block, half),
            pltpu.VMEM((places,) + block, half),
            pltpu.VMEM((rows * row_cap,) + block, half),
            pltpu.VMEM((rows * row_cap,) + block, half),
            pltpu.VMEM((rows * row_cap,) + block, half),
            pltpu.VMEM((ITERS, places) + block, half),
            pltpu.VMEM((ITERS, rows * row_cap) + block, half),
            pltpu.VMEM((ITERS, places) + block, half),
            pltpu.SemaphoreType.DMA((5,)),
            pltpu.SemaphoreType.DMA((rows + cols,)),
            pltpu.SemaphoreType.DMA((rows + cols,)),
            pltpu.SemaphoreType.DMA((ITERS, rows + cols)),
            pltpu.SemaphoreType.DMA((ITERS, rows + cols)),
        ],
        compiler_params=pltpu.CompilerParams(
            collective_id=0, has_side_effects=True, vmem_limit_bytes=52 * 1024 * 1024
        ),
        name="sweeps",
    )(
        table,
        amplitudes,
        meta,
        row_fock,
        col_fock,
        pair_occ.reshape(-1),
        fock_occ,
        exchange_ints,
        row_intersection,
        col_intersection,
        pno_energy.reshape(pairs, 1, width),
    )


def solution(mesh):
    return jax.shard_map(
        body,
        mesh=mesh,
        in_specs=(
            P(("oi", "oj"), None, None),
            P(("oi", "oj"), None, None),
            P(("oi", "oj"), None, None),
            P(("oi", "oj"), None, None),
            P(("oi", "oj"), None),
            P(("oi", "oj")),
            P(("oi", "oj")),
            P(("oi", "oj"), None),
            P(),
            P(("oi", "oj"), None),
            P(("oi", "oj")),
            P(("oi", "oj"), None),
            P(("oi", "oj")),
        ),
        out_specs=(P(("oi", "oj"), None, None), P(("oi", "oj"), None, None)),
        check_vma=False,
    )
```

time: 182 us -> 80 us (0.44)
  waiting for transfers between devices: 90.1 us -> 0 us
  Pallas kernels: 0 us -> 75 us
  starting transfers between devices: 36.2 us -> 0 us
  local copies, waits for them, and re-layouts: 26.8 us -> 4.1 us
  matrix products: 20.5 us -> 0 us
  other arithmetic: 5.63 us -> 0 us
    all_to_all x8 -> x0, waiting for transfers between devices: 90.1 us -> none  [the longest x3 45.5 us: body(): lax.all_to_all(current[col_wanted], 'oi', split_axis=0, concat_axis=0, ti...]
    pallas_call x0 -> x2, Pallas kernels: none -> 75 us  [the longest x1 73 us: body(): pl.pallas_call(functools.partial(sweep_kernel, rows, cols, row_cap, col_c...]
    all_to_all x8 -> x0, starting transfers between devices: 36.2 us -> none  [the longest x3 13.3 us: body(): lax.all_to_all(current[row_wanted], 'oj', split_axis=0, concat_axis=0, ti...]
    gather x12 -> x0, local copies, waits for them, and re-layouts: 23.3 us -> none  [the longest x3 7.33 us: body(): col_fetched.reshape(-1, width, width)[col_target]]
    dot_general x6 -> x0, matrix products: 20.5 us -> none  [couple(): jnp.einsum('pac,pdc->pad', first, intersection, preferred_element_type=jn...]
    unnamed x19 -> x17, local copies, waits for them, and re-layouts: 0.13 us -> 4.01 us
    reduce_sum x3 -> x0, other arithmetic: 2.46 us -> none  [the longest x2 1.67 us: layout(): before = jnp.sum((jnp.cumsum(marker, axis=0) - marker) * marker, axis=1)]
  transfers between devices with their start and end apart: 8 -> 0, of which waited for: 8 -> 0; matrix products, arithmetic and copies ran while one was open for 15% -> 0% of each run, Pallas kernels for 0% -> 0%
where the time goes in v1:
time: 80 us; the launch traced here: 79.8 us
  Pallas kernels  75 us (94%)
  local copies, waits for them, and re-layouts  4.1 us (5%)
    pallas_call x1, Pallas kernels, body(): pl.pallas_call(functools.partial(sweep_kernel, rows, cols, row_cap, col_c...  73 us
    unnamed x17, local copies, waits for them, and re-layouts  4.01 us
    pallas_call x1, Pallas kernels, body(): pl.pallas_call(functools.partial(plan_kernel, rows, cols, row_cap, col_ca...  1.96 us

profile of v1, /device:TPU:0, one launch (start us, length us, event | category | flops | bytes accessed | tf_op | source)
XLA Modules:
  0.0 79.8 jit_solution(16573863708426103838)
XLA Ops:
  0.6 2.0 %plan.1 = (s32[12,1,128]{2,1,0:T(1,128)}, s32[3,128]{1,0:T(4,128)}) custom-call(s32[24]{0:T(128)} %bitcast.4, s32[24]{0:T(128)} %row_slot.1, s32[24]{0:T(128)} %bitcast.5, s32[24]{0:T(128)} %col_slot.1), custom_call_target="tpu_custom_call" | custom-call | tf_op jit(solution)/shard_map/plan/pallas_call | solution.py:274
  2.6 0.0 copy-start.6
  2.6 0.7 copy-done.6
  3.3 0.0 copy-start.1
  3.3 0.1 copy.16
  3.4 0.0 copy-start.2
  3.4 0.0 copy-start.3
  3.4 0.0 copy-start.4
  3.4 0.0 copy-start.5
  3.4 0.1 reshape.18.pair_occ
  3.5 0.5 copy-done.1
  4.0 0.1 copy-done.2
  4.1 0.0 copy-done.3
  4.1 0.0 copy-done.4
  4.1 0.0 copy-done.5
  4.1 0.0 copy-start
  4.1 0.9 %copy-done = f32[20000]{0:T(1024)S(1)} copy-done((f32[20000]{0:T(1024)S(1)}, f32[20000]{0:T(1024)}, u32[]{:S(2)}) %copy-start) | copy-done | bytes 80024
  5.0 73.0 %sweeps.1 = (bf16[24,128,128]{2,1,0:T(8,128)(2,1)S(1)}, bf16[24,128,128]{2,1,0:T(8,128)(2,1)S(1)}) custom-call(s32[12,1,128]{2,1,0:T(1,128)S(1)} %copy-done.2, bf16[24,128,128]{2,1,0:T(8,128)(2,1)} %amps.1, s32[3,128]{1,0:T(4,128)S(1)} %copy-done.3, f32[24]{0:T(128)S(1)} %copy-done.4, f32[24]{0:T(128)S(1)} %copy-done.5, s32[48]{0:T(128)S(1)} %reshape.18.pair_occ, ...), custom_call_target="tpu_custom_call" | custom-call | tf_op jit(solution)/shard_map/sweeps/pallas_call | solution.py:288
  78.0 0.9 %copy.19 = bf16[24,128,128]{2,1,0:T(8,128)(2,1)} copy(bf16[24,128,128]{2,1,0:T(8,128)(2,1)S(1)} %get-tuple-element.8) | data formatting | bytes 1572864
  78.9 0.9 %copy.20 = bf16[24,128,128]{2,1,0:T(8,128)(2,1)} copy(bf16[24,128,128]{2,1,0:T(8,128)(2,1)S(1)} %get-tuple-element.9) | data formatting | bytes 1572864
Async XLA Ops:
  2.6 0.7 copy-start.6
  3.3 0.7 copy-start.1
  3.4 0.7 copy-start.2
  3.4 0.7 copy-start.3
  3.4 0.7 copy-start.4
  3.4 0.7 copy-start.5
  4.1 0.9 %copy-start = (f32[20000]{0:T(1024)S(1)}, f32[20000]{0:T(1024)}, u32[]{:S(2)}) copy-start(f32[20000]{0:T(1024)} %fock_hbm.1) | copy-start | bytes 240004

commit v2 on v1

v2 whole, which is shorter than its diff:
```python
import functools
import jax
import jax.numpy as jnp
from jax import lax
from jax.experimental import pallas as pl
from jax.experimental.pallas import tpu as pltpu
from jax.sharding import PartitionSpec as P

ITERS = 3
LANES = 128


def flip(me, step):
    out = me
    bit = 1
    while bit <= step:
        if step & bit:
            out = out + bit * (1 - 2 * ((me // bit) % 2))
        bit *= 2
    return out


def grouped(peer, me):
    group = (peer ^ me).astype(jnp.float32)
    along = jnp.broadcast_to(group, (LANES, LANES))
    earlier = lax.broadcasted_iota(jnp.int32, (LANES, LANES), 0) < lax.broadcasted_iota(
        jnp.int32, (LANES, LANES), 1
    )
    same = jnp.where((along.T == along) & earlier, 1.0, 0.0)
    return group, jnp.sum(same, axis=0, keepdims=True)


def bounded(values, count):
    return jnp.minimum(jnp.maximum(values.astype(jnp.int32), 0), count - 1)


def listed(group, before, values, count, cap, pairs):
    tall = -(-count // 8) * 8
    which = lax.broadcasted_iota(jnp.int32, (tall, LANES), 0).astype(jnp.float32)
    lane = lax.broadcasted_iota(jnp.int32, (tall, LANES), 1)
    mine = group == which
    out = jnp.zeros((tall, LANES), jnp.float32)
    for t in range(cap):
        one = jnp.sum(jnp.where(mine & (before == t), values, 0.0), axis=1, keepdims=True)
        out = jnp.where(lane == t, one, out)
    return bounded(out, pairs)


def sweep_kernel(
    rows,
    cols,
    row_cap,
    col_cap,
    row_peer_hbm,
    row_slot_hbm,
    col_peer_hbm,
    col_slot_hbm,
    amps_hbm,
    row_fock_hbm,
    col_fock_hbm,
    pair_occ_hbm,
    fock_hbm,
    ints_hbm,
    row_over_hbm,
    col_over_hbm,
    energy_hbm,
    new_out,
    res_out,
    short,
    long,
    table,
    places_in,
    meta,
    row_fock,
    col_fock,
    pair_occ,
    fock,
    amps,
    ints,
    row_over,
    col_over,
    energy,
    want_in,
    want,
    denom,
    inverse,
    partial,
    current,
    res_sorted,
    row_got_0,
    row_got_1,
    row_got_2,
    col_got,
    row_send,
    col_send,
    local_sem,
    table_send_sem,
    table_recv_sem,
    row_send_sem,
    row_recv_sem,
    col_send_sem,
    col_recv_sem,
):
    row_got = (row_got_0, row_got_1, row_got_2)
    places = cols * col_cap
    pairs = amps.shape[0]
    width = amps.shape[1]
    row_me, col_me = lax.axis_index("oj"), lax.axis_index("oi")
    groups = [g for g in range(rows + cols) if g not in (0, rows)]
    place_at, from_at = cols, cols + 1

    def peer(g):
        if g < rows:
            return {"oj": flip(row_me, g)}
        return {"oi": flip(col_me, g - rows)}

    def local(source, target, i):
        return pltpu.make_async_copy(source, target, local_sem.at[i])

    small = [
        local(source, short.at[i], i)
        for i, source in enumerate((row_peer_hbm, row_slot_hbm, col_peer_hbm, col_slot_hbm))
    ]
    first_load = local(amps_hbm, amps, 4)
    loads = [
        local(source, target, 5 + i)
        for i, (source, target) in enumerate(
            (
                (energy_hbm, energy),
                (row_fock_hbm, row_fock),
                (col_fock_hbm, col_fock),
                (pair_occ_hbm, pair_occ),
                (fock_hbm, fock),
                (row_over_hbm, row_over),
                (col_over_hbm, col_over),
                (ints_hbm, ints),
            )
        )
    ]
    for load in small:
        load.start()
    barrier = pltpu.get_barrier_semaphore()
    for g in groups:
        pl.semaphore_signal(
            barrier, inc=1, device_id=peer(g), device_id_type=pl.DeviceIdType.MESH
        )
    first_load.start()
    for load in loads:
        load.start()
    long[...] = jnp.full(long.shape, 1 << 20, jnp.int32)
    for load in small:
        load.wait()
    for i in range(4):
        long[i, :, 0:pairs] = short[i]
    row_group, row_before = grouped(long[0], row_me)
    col_group_of, col_before = grouped(long[2], col_me)
    row_asked = listed(row_group, row_before, long[1].astype(jnp.float32), rows, row_cap, pairs)
    col_asked = listed(col_group_of, col_before, long[3].astype(jnp.float32), cols, col_cap, pairs)
    for g in range(rows):
        table[g] = row_asked[g : g + 1]
    for g in range(cols):
        table[rows + g] = col_asked[g : g + 1]
    pl.semaphore_wait(barrier, len(groups))
    asks = []
    for g in groups:
        ask = pltpu.make_async_remote_copy(
            src_ref=table.at[g],
            dst_ref=want_in.at[g],
            send_sem=table_send_sem.at[g],
            recv_sem=table_recv_sem.at[g],
            device_id=peer(g),
            device_id_type=pl.DeviceIdType.MESH,
        )
        ask.start()
        asks.append(ask)
    want_in[0] = table[0]
    want_in[rows] = table[rows]
    pair_ids = lax.broadcasted_iota(jnp.int32, (1, LANES), 1).astype(jnp.float32)
    order = listed(col_group_of, col_before, pair_ids, cols, col_cap, pairs)
    for h in range(cols):
        places_in[h] = order[h : h + 1]
    places_in[place_at] = bounded(col_group_of * col_cap + col_before, places)
    places_in[from_at] = bounded(row_group * row_cap + row_before, rows * row_cap)
    move_places = local(places_in, meta, 13)
    move_places.start()
    move_places.wait()
    first_load.wait()
    for ask in asks:
        ask.wait()
    move = local(want_in, want, 14)
    move.start()
    move.wait()

    def row_copy(sweep, g):
        here = pl.ds(g * row_cap, row_cap)
        return pltpu.make_async_remote_copy(
            src_ref=row_send.at[sweep, here],
            dst_ref=row_got[sweep].at[here],
            send_sem=row_send_sem.at[sweep, g],
            recv_sem=row_recv_sem.at[sweep, g],
            device_id=peer(g),
            device_id_type=pl.DeviceIdType.MESH,
        )

    def col_copy(sweep, h, t):
        here = pl.ds(h * col_cap + t, 1)
        return pltpu.make_async_remote_copy(
            src_ref=col_send.at[sweep, here],
            dst_ref=col_got.at[sweep, here],
            send_sem=col_send_sem.at[sweep, h * col_cap + t],
            recv_sem=col_recv_sem.at[sweep, h * col_cap + t],
            device_id=peer(rows + h),
            device_id_type=pl.DeviceIdType.MESH,
        )

    def wait_sent(sweep):
        for g in range(1, rows):
            row_copy(sweep, g).wait_send()
        for h in range(1, cols):
            for t in range(col_cap):
                col_copy(sweep, h, t).wait_send()

    def dot(a, b, contract):
        return lax.dot_general(
            a, b, (((1,), (contract,)), ((), ())), preferred_element_type=jnp.float32
        )

    def couple(blocks, overs):
        firsts = [dot(o, b, 0).astype(jnp.bfloat16) for o, b in zip(overs, blocks)]
        return [dot(f, o, 1) for f, o in zip(firsts, overs)]

    for sweep in range(ITERS):
        held = (sweep + 1) % 2

        def taken(slot):
            if sweep == 0:
                return amps[slot]
            return current[held, meta[place_at, 0, slot]]

        def send_rows(g):
            for t in range(row_cap):
                row_send[sweep, g * row_cap + t] = taken(want[g, 0, t])
            row_copy(sweep, g).start()

        row_next = 1
        for t in range(col_cap):
            for h in range(cols - 1, 0, -1):
                col_send[sweep, h * col_cap + t] = taken(want[rows + h, 0, t])
                col_copy(sweep, h, t).start()
            row_end = 1 + (rows - 1) * (t + 1) // col_cap
            for g in range(row_next, row_end):
                send_rows(g)
            row_next = row_end
        for t in range(col_cap):
            col_got[sweep, t] = taken(want[rows, 0, t])
        for t in range(row_cap):
            row_got[sweep][t] = taken(want[0, 0, t])

        if sweep == 0:
            for load in loads:
                load.wait()

            @pl.loop(0, cols)
            def _(h):
                for t in range(col_cap):
                    p = meta[h, 0, t]
                    occupied = fock[pair_occ[0, p]] + fock[pair_occ[1, p]]
                    across = jnp.broadcast_to(energy[p], (width, width))
                    value = across + across.T - occupied
                    denom[h * col_cap + t] = value
                    inverse[h * col_cap + t] = 1.0 / value
        else:
            wait_sent(sweep - 1)

        for g in range(1, rows):
            row_copy(sweep, g).wait_recv()

        @pl.loop(0, cols)
        def _(h):
            who = [meta[h, 0, t] for t in range(col_cap)]
            overs = [row_over[p] for p in who]
            blocks = [row_got[sweep][meta[from_at, 0, p]] for p in who]
            for t, (p, term) in enumerate(zip(who, couple(blocks, overs))):
                partial[h * col_cap + t] = row_fock[p] * term - ints[p].astype(jnp.float32)

        def col_part(at):
            who = [meta[h, 0, t] for h, t in at]
            overs = [col_over[p] for p in who]
            keys = [h * col_cap + t for h, t in at]
            blocks = [col_got[sweep, k] for k in keys]
            for k, p, term in zip(keys, who, couple(blocks, overs)):
                total = partial[k] + col_fock[p] * term
                if sweep == ITERS - 1:
                    own = current[held, k].astype(jnp.float32)
                    res_sorted[k] = (denom[k] * own - total).astype(jnp.bfloat16)
                current[sweep % 2, k] = (total * inverse[k]).astype(jnp.bfloat16)

        near = min(2, cols)
        for h in range(near):
            if h:
                for t in range(col_cap):
                    col_copy(sweep, h, t).wait_recv()
            col_part([(h, t) for t in range(col_cap)])
        for t in range(col_cap):
            for h in range(near, cols):
                col_copy(sweep, h, t).wait_recv()
            col_part([(h, t) for h in range(near, cols)])

    for p in range(pairs):
        place = meta[place_at, 0, p]
        new_out[p] = current[(ITERS - 1) % 2, place]
        res_out[p] = res_sorted[place]
    wait_sent(ITERS - 1)


def body(
    amplitudes,
    exchange_ints,
    row_intersection,
    col_intersection,
    pno_energy,
    row_fock,
    col_fock,
    pair_occ,
    fock_occ,
    row_peer,
    row_slot,
    col_peer,
    col_slot,
):
    pairs, width, _ = amplitudes.shape
    rows, cols = lax.axis_size("oj"), lax.axis_size("oi")
    row_cap = max(2, (pairs + rows - 1) // rows + 1)
    col_cap = max(2, (pairs + cols - 1) // cols + 1)
    places = cols * col_cap
    wide = jax.ShapeDtypeStruct(amplitudes.shape, jnp.bfloat16)
    block = (width, width)
    half, full, whole = jnp.bfloat16, jnp.float32, jnp.int32
    vmem, smem = pltpu.VMEM, pltpu.SMEM
    return pl.pallas_call(
        functools.partial(sweep_kernel, rows, cols, row_cap, col_cap),
        out_shape=(wide, wide),
        in_specs=[pl.BlockSpec(memory_space=pltpu.HBM)] * 13,
        out_specs=(pl.BlockSpec(memory_space=vmem),) * 2,
        scratch_shapes=[
            vmem((4, 1, pairs), whole),
            vmem((4, 1, LANES), whole),
            vmem((rows + cols, 1, LANES), whole),
            vmem((cols + 2, 1, LANES), whole),
            smem((cols + 2, 1, LANES), whole),
            smem((pairs,), full),
            smem((pairs,), full),
            smem((2, pairs), whole),
            smem(fock_occ.shape, full),
            vmem(amplitudes.shape, half),
            vmem(amplitudes.shape, half),
            vmem(amplitudes.shape, half),
            vmem(amplitudes.shape, half),
            vmem((pairs, 1, width), full),
            vmem((rows + cols, 1, LANES), whole),
            smem((rows + cols, 1, LANES), whole),
            vmem((places,) + block, full),
            vmem((places,) + block, full),
            vmem((places,) + block, full),
            vmem((2, places) + block, half),
            vmem((places,) + block, half),
            vmem((rows * row_cap,) + block, half),
            vmem((rows * row_cap,) + block, half),
            vmem((rows * row_cap,) + block, half),
            vmem((ITERS, places) + block, half),
            vmem((ITERS, rows * row_cap) + block, half),
            vmem((ITERS, places) + block, half),
            pltpu.SemaphoreType.DMA((15,)),
            pltpu.SemaphoreType.DMA((rows + cols,)),
            pltpu.SemaphoreType.DMA((rows + cols,)),
            pltpu.SemaphoreType.DMA((ITERS, rows)),
            pltpu.SemaphoreType.DMA((ITERS, rows)),
            pltpu.SemaphoreType.DMA((ITERS, places)),
            pltpu.SemaphoreType.DMA((ITERS, places)),
        ],
        compiler_params=pltpu.CompilerParams(
            collective_id=0, has_side_effects=True, vmem_limit_bytes=60 * 1024 * 1024
        ),
        name="sweeps",
    )(
        row_peer.reshape(1, pairs),
        row_slot.reshape(1, pairs),
        col_peer.reshape(1, pairs),
        col_slot.reshape(1, pairs),
        amplitudes,
        row_fock,
        col_fock,
        pair_occ.T,
        fock_occ,
        exchange_ints,
        row_intersection,
        col_intersection,
        pno_energy.reshape(pairs, 1, width),
    )


def solution(mesh):
    return jax.shard_map(
        body,
        mesh=mesh,
        in_specs=(
            P(("oi", "oj"), None, None),
            P(("oi", "oj"), None, None),
            P(("oi", "oj"), None, None),
            P(("oi", "oj"), None, None),
            P(("oi", "oj"), None),
            P(("oi", "oj")),
            P(("oi", "oj")),
            P(("oi", "oj"), None),
            P(),
            P(("oi", "oj"), None),
            P(("oi", "oj")),
            P(("oi", "oj"), None),
            P(("oi", "oj")),
        ),
        out_specs=(P(("oi", "oj"), None, None), P(("oi", "oj"), None, None)),
        check_vma=False,
    )
```

time: 80 us -> 78.9 us (0.986)
  local copies, waits for them, and re-layouts: 4.1 us -> 3.04 us
    pallas_call x1, Pallas kernels: 73 us -> 75 us  [body(): pl.pallas_call(functools.partial(sweep_kernel, rows, cols, row_cap, col_c...]
    pallas_call x1 -> x0, Pallas kernels: 1.96 us -> none  [body(): pl.pallas_call(functools.partial(plan_kernel, rows, cols, row_cap, col_ca...]
    unnamed x17 -> x4, local copies, waits for them, and re-layouts: 4.01 us -> 3.04 us
where the time goes in v2:
time: 78.9 us; the launch traced here: 78.7 us
  Pallas kernels  75 us (95%)
  local copies, waits for them, and re-layouts  3.04 us (4%)
    pallas_call x1, Pallas kernels, body(): pl.pallas_call(functools.partial(sweep_kernel, rows, cols, row_cap, col_c...  75 us
    unnamed x4, local copies, waits for them, and re-layouts  3.04 us

profile of v2, /device:TPU:0, one launch (start us, length us, event | category | flops | bytes accessed | tf_op | source)
XLA Modules:
  0.0 78.7 jit_solution(7205467885950334396)
XLA Ops:
  0.6 75.0 %sweeps.1 = (bf16[24,128,128]{2,1,0:T(8,128)(2,1)}, bf16[24,128,128]{2,1,0:T(8,128)(2,1)}) custom-call(s32[1,24]{1,0:T(1,128)} %bitcast.8, s32[1,24]{1,0:T(1,128)} %bitcast.9, s32[1,24]{1,0:T(1,128)} %bitcast.10, s32[1,24]{1,0:T(1,128)} %bitcast.11, bf16[24,128,128]{2,1,0:T(8,128)(2,1)} %amps_hbm.1, f32[24]{0:T(128)} %row_fock_hbm.1, f32[24]{0:T(128)} %col_fock_hbm.1, ...), custom_call_target="tpu_custom_call" | custom-call | tf_op jit(solution)/shard_map/sweeps/pallas_call | solution.py:340
  75.7 0.0 copy-start
  75.7 2.2 %copy.17 = bf16[24,128,128]{2,1,0:T(8,128)(2,1)} copy(bf16[24,128,128]{2,1,0:T(8,128)(2,1)} %get-tuple-element.4) | data formatting | bytes 1572864
  77.8 0.0 copy-done
  77.8 0.9 %copy.18 = bf16[24,128,128]{2,1,0:T(8,128)(2,1)} copy(bf16[24,128,128]{2,1,0:T(8,128)(2,1)S(1)} %copy-done) | data formatting | bytes 1572864
Async XLA Ops:
  75.7 2.2 %copy-start = (bf16[24,128,128]{2,1,0:T(8,128)(2,1)S(1)}, bf16[24,128,128]{2,1,0:T(8,128)(2,1)}, u32[]{:S(2)}) copy-start(bf16[24,128,128]{2,1,0:T(8,128)(2,1)} %get-tuple-element.5) | copy-start | bytes 2359300

commit v3 on v2

--- a/solution.py
+++ b/solution.py
@@ -152,18 +152,13 @@
         load.wait()
     for i in range(4):
         long[i, :, 0:pairs] = short[i]
-    row_group, row_before = grouped(long[0], row_me)
     col_group_of, col_before = grouped(long[2], col_me)
-    row_asked = listed(row_group, row_before, long[1].astype(jnp.float32), rows, row_cap, pairs)
     col_asked = listed(col_group_of, col_before, long[3].astype(jnp.float32), cols, col_cap, pairs)
-    for g in range(rows):
-        table[g] = row_asked[g : g + 1]
     for g in range(cols):
         table[rows + g] = col_asked[g : g + 1]
-    pl.semaphore_wait(barrier, len(groups))
-    asks = []
-    for g in groups:
-        ask = pltpu.make_async_remote_copy(
+
+    def ask(g):
+        return pltpu.make_async_remote_copy(
             src_ref=table.at[g],
             dst_ref=want_in.at[g],
             send_sem=table_send_sem.at[g],
@@ -171,25 +166,40 @@
             device_id=peer(g),
             device_id_type=pl.DeviceIdType.MESH,
         )
-        ask.start()
-        asks.append(ask)
+
+    pl.semaphore_wait(barrier, len(groups))
+    for g in range(rows + 1, rows + cols):
+        ask(g).start()
+    row_group, row_before = grouped(long[0], row_me)
+    row_asked = listed(row_group, row_before, long[1].astype(jnp.float32), rows, row_cap, pairs)
+    for g in range(rows):
+        table[g] = row_asked[g : g + 1]
+    for g in range(1, rows):
+        ask(g).start()
     want_in[0] = table[0]
     want_in[rows] = table[rows]
-    pair_ids = lax.broadcasted_iota(jnp.int32, (1, LANES), 1).astype(jnp.float32)
-    order = listed(col_group_of, col_before, pair_ids, cols, col_cap, pairs)
-    for h in range(cols):
-        places_in[h] = order[h : h + 1]
-    places_in[place_at] = bounded(col_group_of * col_cap + col_before, places)
-    places_in[from_at] = bounded(row_group * row_cap + row_before, rows * row_cap)
-    move_places = local(places_in, meta, 13)
-    move_places.start()
-    move_places.wait()
     first_load.wait()
-    for ask in asks:
-        ask.wait()
-    move = local(want_in, want, 14)
-    move.start()
-    move.wait()
+
+    def take_asked(first, count, i):
+        for g in range(first + 1, first + count):
+            ask(g).wait()
+        here = pl.ds(first, count)
+        move = local(want_in.at[here], want.at[here], i)
+        move.start()
+        return move
+
+    take_asked(rows, cols, 14).wait()
+
+    def place_pairs():
+        pair_ids = lax.broadcasted_iota(jnp.int32, (1, LANES), 1).astype(jnp.float32)
+        order = listed(col_group_of, col_before, pair_ids, cols, col_cap, pairs)
+        for h in range(cols):
+            places_in[h] = order[h : h + 1]
+        places_in[place_at] = bounded(col_group_of * col_cap + col_before, places)
+        places_in[from_at] = bounded(row_group * row_cap + row_before, rows * row_cap)
+        move = local(places_in, meta, 13)
+        move.start()
+        return move
 
     def row_copy(sweep, g):
         here = pl.ds(g * row_cap, row_cap)
@@ -242,21 +252,33 @@
                 row_send[sweep, g * row_cap + t] = taken(want[g, 0, t])
             row_copy(sweep, g).start()
 
-        row_next = 1
-        for t in range(col_cap):
+        def send_cols(t):
             for h in range(cols - 1, 0, -1):
                 col_send[sweep, h * col_cap + t] = taken(want[rows + h, 0, t])
                 col_copy(sweep, h, t).start()
-            row_end = 1 + (rows - 1) * (t + 1) // col_cap
-            for g in range(row_next, row_end):
+
+        if sweep == 0:
+            for t in range(col_cap):
+                send_cols(t)
+            take_asked(0, rows, 15).wait()
+            for g in range(1, rows):
                 send_rows(g)
-            row_next = row_end
+            moved = place_pairs()
+        else:
+            row_next = 1
+            for t in range(col_cap):
+                send_cols(t)
+                row_end = 1 + (rows - 1) * (t + 1) // col_cap
+                for g in range(row_next, row_end):
+                    send_rows(g)
+                row_next = row_end
         for t in range(col_cap):
             col_got[sweep, t] = taken(want[rows, 0, t])
         for t in range(row_cap):
             row_got[sweep][t] = taken(want[0, 0, t])
 
         if sweep == 0:
+            moved.wait()
             for load in loads:
                 load.wait()
 
@@ -311,6 +333,22 @@
         new_out[p] = current[(ITERS - 1) % 2, place]
         res_out[p] = res_sorted[place]
     wait_sent(ITERS - 1)
+
+
+def store_kernel(new_in, res_in, new_out, res_out, sem):
+    pairs, parts = new_in.shape[0], sem.shape[1]
+    copies = []
+    for i, (source, target) in enumerate(((new_in, new_out), (res_in, res_out))):
+        for part in range(parts):
+            first, end = pairs * part // parts, pairs * (part + 1) // parts
+            here = pl.ds(first, end - first)
+            copies.append(
+                pltpu.make_async_copy(source.at[here], target.at[here], sem.at[i, part])
+            )
+    for copy in copies:
+        copy.start()
+    for copy in copies:
+        copy.wait()
 
 
 def body(
@@ -337,9 +375,9 @@
     block = (width, width)
     half, full, whole = jnp.bfloat16, jnp.float32, jnp.int32
     vmem, smem = pltpu.VMEM, pltpu.SMEM
-    return pl.pallas_call(
+    new, res = pl.pallas_call(
         functools.partial(sweep_kernel, rows, cols, row_cap, col_cap),
-        out_shape=(wide, wide),
+        out_shape=(vmem(amplitudes.shape, half),) * 2,
         in_specs=[pl.BlockSpec(memory_space=pltpu.HBM)] * 13,
         out_specs=(pl.BlockSpec(memory_space=vmem),) * 2,
         scratch_shapes=[
@@ -370,7 +408,7 @@
             vmem((ITERS, places) + block, half),
             vmem((ITERS, rows * row_cap) + block, half),
             vmem((ITERS, places) + block, half),
-            pltpu.SemaphoreType.DMA((15,)),
+            pltpu.SemaphoreType.DMA((16,)),
             pltpu.SemaphoreType.DMA((rows + cols,)),
             pltpu.SemaphoreType.DMA((rows + cols,)),
             pltpu.SemaphoreType.DMA((ITERS, rows)),
@@ -379,10 +417,11 @@
             pltpu.SemaphoreType.DMA((ITERS, places)),
         ],
         compiler_params=pltpu.CompilerParams(
-            collective_id=0, has_side_effects=True, vmem_limit_bytes=60 * 1024 * 1024
+            collective_id=0, has_side_effects=True, vmem_limit_bytes=48 * 1024 * 1024
         ),
         name="sweeps",
     )(
+        *(pltpu.with_memory_space_constraint(x, pltpu.HBM) for x in (
         row_peer.reshape(1, pairs),
         row_slot.reshape(1, pairs),
         col_peer.reshape(1, pairs),
@@ -396,7 +435,16 @@
         row_intersection,
         col_intersection,
         pno_energy.reshape(pairs, 1, width),
+        ))
     )
+    return pl.pallas_call(
+        store_kernel,
+        out_shape=(wide, wide),
+        in_specs=[pl.BlockSpec(memory_space=vmem)] * 2,
+        out_specs=(pl.BlockSpec(memory_space=pltpu.HBM),) * 2,
+        scratch_shapes=[pltpu.SemaphoreType.DMA((2, 4))],
+        name="store",
+    )(new, res)
 
 
 def solution(mesh):

time: 78.9 us -> 78 us (0.989)
  local copies, waits for them, and re-layouts: 3.04 us -> 1.79 us
    pallas_call x0 -> x1, Pallas kernels: none -> 2.57 us  [body(): pl.pallas_call(store_kernel, out_shape=(wide, wide), in_specs=[pl.BlockSp...]
    pallas_call x1, Pallas kernels: 75 us -> 72.8 us  [body(): pl.pallas_call(functools.partial(sweep_kernel, rows, cols, row_cap, col_c...]
    unnamed x4, local copies, waits for them, and re-layouts: 3.04 us -> 1.79 us
where the time goes in v3:
time: 78 us; the launch traced here: 77.8 us
  Pallas kernels  75.4 us (97%)
  local copies, waits for them, and re-layouts  1.79 us (2%)
    pallas_call x1, Pallas kernels, body(): pl.pallas_call(functools.partial(sweep_kernel, rows, cols, row_cap, col_c...  72.8 us
    pallas_call x1, Pallas kernels, body(): pl.pallas_call(store_kernel, out_shape=(wide, wide), in_specs=[pl.BlockSp...  2.57 us
    unnamed x4, local copies, waits for them, and re-layouts  1.79 us

profile of v3, /device:TPU:0, one launch (start us, length us, event | category | flops | bytes accessed | tf_op | source)
XLA Modules:
  0.0 77.8 jit_solution(11069539042658621912)
XLA Ops:
  0.6 72.8 %sweeps.1 = (bf16[24,128,128]{2,1,0:T(8,128)(2,1)S(1)}, bf16[24,128,128]{2,1,0:T(8,128)(2,1)S(1)}) custom-call(s32[1,24]{1,0:T(1,128)} %bitcast.8, s32[1,24]{1,0:T(1,128)} %bitcast.9, s32[1,24]{1,0:T(1,128)} %bitcast.10, s32[1,24]{1,0:T(1,128)} %bitcast.11, bf16[24,128,128]{2,1,0:T(8,128)(2,1)} %amps_hbm.1, f32[24]{0:T(128)} %row_fock_hbm.1, ...), custom_call_target="tpu_custom_call" | custom-call | tf_op jit(solution)/shard_map/sweeps/pallas_call | solution.py:378
  73.5 0.0 copy-start
  73.5 0.9 %copy-done = bf16[24,128,128]{2,1,0:T(8,128)(2,1)} copy-done((bf16[24,128,128]{2,1,0:T(8,128)(2,1)}, bf16[24,128,128]{2,1,0:T(8,128)(2,1)S(1)}, u32[]{:S(2)}) %copy-start) | copy-done | bytes 786456
  74.3 0.0 copy-start.1
  74.3 0.9 %copy-done.1 = bf16[24,128,128]{2,1,0:T(8,128)(2,1)} copy-done((bf16[24,128,128]{2,1,0:T(8,128)(2,1)}, bf16[24,128,128]{2,1,0:T(8,128)(2,1)S(1)}, u32[]{:S(2)}) %copy-start.1) | copy-done | bytes 786456
  75.2 2.6 %store.1 = (bf16[24,128,128]{2,1,0:T(8,128)(2,1)}, bf16[24,128,128]{2,1,0:T(8,128)(2,1)}) custom-call(bf16[24,128,128]{2,1,0:T(8,128)(2,1)} %copy-done, bf16[24,128,128]{2,1,0:T(8,128)(2,1)} %copy-done.1), custom_call_target="tpu_custom_call" | custom-call | tf_op jit(solution)/shard_map/store/pallas_call | solution.py:440
Async XLA Ops:
  73.5 0.9 %copy-start = (bf16[24,128,128]{2,1,0:T(8,128)(2,1)}, bf16[24,128,128]{2,1,0:T(8,128)(2,1)S(1)}, u32[]{:S(2)}) copy-start(bf16[24,128,128]{2,1,0:T(8,128)(2,1)S(1)} %get-tuple-element.4.new_in) | copy-start | bytes 2359300
  74.3 0.9 %copy-start.1 = (bf16[24,128,128]{2,1,0:T(8,128)(2,1)}, bf16[24,128,128]{2,1,0:T(8,128)(2,1)S(1)}, u32[]{:S(2)}) copy-start(bf16[24,128,128]{2,1,0:T(8,128)(2,1)S(1)} %get-tuple-element.5.res_in) | copy-start | bytes 2359300

commit v4 on v3

--- a/solution.py
+++ b/solution.py
@@ -443,6 +443,7 @@
         in_specs=[pl.BlockSpec(memory_space=vmem)] * 2,
         out_specs=(pl.BlockSpec(memory_space=pltpu.HBM),) * 2,
         scratch_shapes=[pltpu.SemaphoreType.DMA((2, 4))],
+        compiler_params=pltpu.CompilerParams(vmem_limit_bytes=1024 * 1024),
         name="store",
     )(new, res)
 

time: 78 us -> 74.8 us (0.959)
  local copies, waits for them, and re-layouts: 1.79 us -> 0 us
  Pallas kernels: 75.4 us -> 74 us
    unnamed x4 -> x0, local copies, waits for them, and re-layouts: 1.79 us -> none
    pallas_call x1, Pallas kernels: 2.57 us -> 1.2 us  [body(): pl.pallas_call(store_kernel, out_shape=(wide, wide), in_specs=[pl.BlockSp...]
where the time goes in v4:
time: 74.8 us; the launch traced here: 74.7 us
  Pallas kernels  74 us (99%)
    pallas_call x1, Pallas kernels, body(): pl.pallas_call(functools.partial(sweep_kernel, rows, cols, row_cap, col_c...  72.8 us

profile of v4, /device:TPU:0, one launch (start us, length us, event | category | flops | bytes accessed | tf_op | source)
XLA Modules:
  0.0 74.7 jit_solution(1189359324130588677)
XLA Ops:
  0.6 72.8 %sweeps.1 = (bf16[24,128,128]{2,1,0:T(8,128)(2,1)S(1)}, bf16[24,128,128]{2,1,0:T(8,128)(2,1)S(1)}) custom-call(s32[1,24]{1,0:T(1,128)} %bitcast.8, s32[1,24]{1,0:T(1,128)} %bitcast.9, s32[1,24]{1,0:T(1,128)} %bitcast.10, s32[1,24]{1,0:T(1,128)} %bitcast.11, bf16[24,128,128]{2,1,0:T(8,128)(2,1)} %amps_hbm.1, f32[24]{0:T(128)} %row_fock_hbm.1, ...), custom_call_target="tpu_custom_call" | custom-call | tf_op jit(solution)/shard_map/sweeps/pallas_call | solution.py:378
  73.5 1.2 %store.1 = (bf16[24,128,128]{2,1,0:T(8,128)(2,1)}, bf16[24,128,128]{2,1,0:T(8,128)(2,1)}) custom-call(bf16[24,128,128]{2,1,0:T(8,128)(2,1)S(1)} %get-tuple-element.4.new_in, bf16[24,128,128]{2,1,0:T(8,128)(2,1)S(1)} %get-tuple-element.5.res_in), custom_call_target="tpu_custom_call" | custom-call | tf_op jit(solution)/shard_map/store/pallas_call | solution.py:440

commit v5 on v4

--- a/solution.py
+++ b/solution.py
@@ -223,10 +223,12 @@
             device_id_type=pl.DeviceIdType.MESH,
         )
 
-    def wait_sent(sweep):
+    near = min(2, cols)
+
+    def wait_sent(sweep, far=True):
         for g in range(1, rows):
             row_copy(sweep, g).wait_send()
-        for h in range(1, cols):
+        for h in range(1, cols if far else near):
             for t in range(col_cap):
                 col_copy(sweep, h, t).wait_send()
 
@@ -257,21 +259,14 @@
                 col_send[sweep, h * col_cap + t] = taken(want[rows + h, 0, t])
                 col_copy(sweep, h, t).start()
 
+        for t in range(col_cap):
+            send_cols(t)
         if sweep == 0:
-            for t in range(col_cap):
-                send_cols(t)
             take_asked(0, rows, 15).wait()
-            for g in range(1, rows):
-                send_rows(g)
+        for g in range(1, rows):
+            send_rows(g)
+        if sweep == 0:
             moved = place_pairs()
-        else:
-            row_next = 1
-            for t in range(col_cap):
-                send_cols(t)
-                row_end = 1 + (rows - 1) * (t + 1) // col_cap
-                for g in range(row_next, row_end):
-                    send_rows(g)
-                row_next = row_end
         for t in range(col_cap):
             col_got[sweep, t] = taken(want[rows, 0, t])
         for t in range(row_cap):
@@ -317,12 +312,13 @@
                     res_sorted[k] = (denom[k] * own - total).astype(jnp.bfloat16)
                 current[sweep % 2, k] = (total * inverse[k]).astype(jnp.bfloat16)
 
-        near = min(2, cols)
         for h in range(near):
             if h:
                 for t in range(col_cap):
                     col_copy(sweep, h, t).wait_recv()
             col_part([(h, t) for t in range(col_cap)])
+        if sweep == ITERS - 1:
+            wait_sent(sweep, far=False)
         for t in range(col_cap):
             for h in range(near, cols):
                 col_copy(sweep, h, t).wait_recv()
@@ -332,7 +328,9 @@
         place = meta[place_at, 0, p]
         new_out[p] = current[(ITERS - 1) % 2, place]
         res_out[p] = res_sorted[place]
-    wait_sent(ITERS - 1)
+    for h in range(near, cols):
+        for t in range(col_cap):
+            col_copy(ITERS - 1, h, t).wait_send()
 
 
 def store_kernel(new_in, res_in, new_out, res_out, sem):

time: 74.8 us -> 74.8 us (level)
  no operation moved by 1% of the time
where the time goes in v5:
time: 74.8 us; the launch traced here: 74.6 us
  Pallas kernels  74 us (99%)
    pallas_call x1, Pallas kernels, body(): pl.pallas_call(functools.partial(sweep_kernel, rows, cols, row_cap, col_c...  72.8 us

profile of v5, /device:TPU:0, one launch (start us, length us, event | category | flops | bytes accessed | tf_op | source)
XLA Modules:
  0.0 74.6 jit_solution(2789552958330607781)
XLA Ops:
  0.6 72.8 %sweeps.1 = (bf16[24,128,128]{2,1,0:T(8,128)(2,1)S(1)}, bf16[24,128,128]{2,1,0:T(8,128)(2,1)S(1)}) custom-call(s32[1,24]{1,0:T(1,128)} %bitcast.8, s32[1,24]{1,0:T(1,128)} %bitcast.9, s32[1,24]{1,0:T(1,128)} %bitcast.10, s32[1,24]{1,0:T(1,128)} %bitcast.11, bf16[24,128,128]{2,1,0:T(8,128)(2,1)} %amps_hbm.1, f32[24]{0:T(128)} %row_fock_hbm.1, ...), custom_call_target="tpu_custom_call" | custom-call | tf_op jit(solution)/shard_map/sweeps/pallas_call | solution.py:376
  73.4 1.2 %store.1 = (bf16[24,128,128]{2,1,0:T(8,128)(2,1)}, bf16[24,128,128]{2,1,0:T(8,128)(2,1)}) custom-call(bf16[24,128,128]{2,1,0:T(8,128)(2,1)S(1)} %get-tuple-element.4.new_in, bf16[24,128,128]{2,1,0:T(8,128)(2,1)S(1)} %get-tuple-element.5.res_in), custom_call_target="tpu_custom_call" | custom-call | tf_op jit(solution)/shard_map/store/pallas_call | solution.py:438
